TPU v7x, 128 devices: a whole 4x4x4 slice. The times are simulated.
128 devices in a mesh: dp: 16 (over x, y), mp: 8 (over z, core).
Axes of the slice: x: 4, y: 4, z: 4, core: 2. Of those that a mesh axis runs over, the one named last changes fastest.
Arguments:
- attn_heads: bfloat16 [2048, 4096], P('dp', 'mp'), may hold values from -6 to 6
- residual: bfloat16 [2048, 4096], P(('dp', 'mp')), may hold values from -24 to 24
- out_weight: bfloat16 [4096, 4096], P('mp'), may hold values from -0.09375 to 0.09375
- norm_gain: float32 [4096], replicated, may hold values from 0.5 to 1.5
- route_ids: int32 [2048, 2], P(('dp', 'mp')), may hold values from 0 to 3, all different within a row; in each aligned block of 16 rows (0 to 15, 16 to 31, ...) at most 12 rows name the same one
- route_weights: float32 [2048, 2], P(('dp', 'mp')), may hold values from 0.1 to 0.9
- gate_weights: bfloat16 [16, 3584, 4096], P('dp', 'mp'), may hold values from -0.09375 to 0.09375
- up_weights: bfloat16 [16, 3584, 4096], P('dp', 'mp'), may hold values from -0.09375 to 0.09375
- down_weights: bfloat16 [16, 3584, 4096], P('dp', 'mp'), may hold values from -0.046875 to 0.046875
Outputs:
- layer_out: bfloat16 [2048, 4096], P(('dp', 'mp'))
Inputs may be any that keep to these rules, and one draw needn't show every extreme that they name: `route_ids`: each row names 2 different experts. Among the 16 rows of one device no expert is named by more than 12 rows, and in every draw some expert is named by exactly 12 rows of some device.
All inputs are finite; a program needn't handle non-finite values.
Results may differ from a plain program's by a relative error of at most 0.017.
Values may be sent and summed in bfloat16 or wider, within the bound.
A program may use at most 192 MiB of HBM per device.

v0:
```python
import jax
import jax.numpy as jnp
from jax import lax
from jax.sharding import PartitionSpec as P

EXPERTS = 4
TOP = 2
CAP = 12


def expert_rows(rows_in, gate_local, up_local, down_local):
    gate = lax.dot_general(
        rows_in, gate_local, (((1,), (1,)), ((), ())), preferred_element_type=jnp.float32
    )
    up = lax.dot_general(
        rows_in, up_local, (((1,), (1,)), ((), ())), preferred_element_type=jnp.float32
    )
    act = (jax.nn.silu(gate) * up).astype(jnp.bfloat16)
    return jnp.dot(act, down_local, preferred_element_type=jnp.float32).astype(jnp.bfloat16)


def body(
    attn_heads,
    residual,
    out_weight,
    norm_gain,
    route_ids,
    route_weights,
    gate_weights,
    up_weights,
    down_weights,
):
    tok_rows = residual.shape[0]
    width = residual.shape[1]
    capacity = CAP
    slots = EXPERTS * capacity
    gate_local = gate_weights[0]
    up_local = up_weights[0]
    down_local = down_weights[0]
    proj = lax.psum_scatter(
        jnp.dot(attn_heads, out_weight, preferred_element_type=jnp.float32).astype(jnp.bfloat16),
        "mp",
        scatter_dimension=0,
        tiled=True,
    ).astype(jnp.float32)
    hidden = residual.astype(jnp.float32) + proj
    square = jnp.mean(hidden * hidden, axis=1, keepdims=True)
    normed = (hidden * lax.rsqrt(square + 1e-05) * norm_gain).astype(jnp.bfloat16)
    onehot = (route_ids[:, :, None] == jnp.arange(EXPERTS, dtype=jnp.int32)).astype(jnp.int32)
    flat = onehot.reshape(-1, EXPERTS)
    before = jnp.cumsum(flat, axis=0) - flat
    slot = jnp.sum(before * flat, axis=1).reshape(tok_rows, TOP)
    target = route_ids * capacity + slot
    matched = target[:, :, None] == jnp.arange(slots, dtype=jnp.int32)
    select = jnp.sum(matched.astype(jnp.int32), axis=1).astype(jnp.bfloat16)
    combine = jnp.sum(jnp.where(matched, route_weights[:, :, None], jnp.float32(0.0)), axis=1)
    packed = lax.dot_general(
        select, normed, (((0,), (0,)), ((), ())), preferred_element_type=jnp.float32
    )
    packed = packed.astype(jnp.bfloat16).reshape(EXPERTS, capacity, width)
    group = lax.axis_size("dp") // EXPERTS
    mp_size = lax.axis_size("mp")
    copies = group * mp_size
    outgoing = jnp.broadcast_to(packed[:, None], (EXPERTS, copies, capacity, width))
    outgoing = outgoing.reshape(EXPERTS * copies, capacity, width)
    received = lax.all_to_all(outgoing, ("dp", "mp"), split_axis=0, concat_axis=0, tiled=True)
    result = expert_rows(received.reshape(-1, width), gate_local, up_local, down_local)
    pieces = result.reshape(received.shape)
    returned = lax.all_to_all(pieces, ("dp", "mp"), split_axis=0, concat_axis=0, tiled=True)
    expert_out = jnp.sum(
        returned.astype(jnp.float32).reshape(EXPERTS, copies, capacity, width), axis=1
    )
    moe = jnp.dot(
        combine,
        expert_out.reshape(slots, width),
        precision=lax.Precision.HIGHEST,
        preferred_element_type=jnp.float32,
    )
    return (hidden + moe).astype(jnp.bfloat16)


def solution(mesh):
    placed = (
        P("dp", "mp"),
        P(("dp", "mp"), None),
        P("mp", None),
        P(),
        P(("dp", "mp"), None),
        P(("dp", "mp"), None),
        P("dp", "mp", None),
        P("dp", "mp", None),
        P("dp", "mp", None),
    )
    return jax.shard_map(
        body, mesh=mesh, in_specs=placed, out_specs=P(("dp", "mp"), None), check_vma=False
    )
```

profile of v0, /device:TPU:50, one launch (start us, length us, event | category | flops | bytes accessed | tf_op | source)
XLA Modules:
  0.0 586.2 jit_solution(12035784486669402794)
XLA Ops:
  6.6 0.9 copy-done
  7.4 3.9 convolution_convert_fusion.1
  11.4 0.1 copy.22
  11.5 0.1 eq.29
  11.7 0.2 select_reduce_fusion.1
  11.9 0.1 reshape.37
  11.9 0.1 copy.23
  12.0 0.1 convert_reduce_fusion.1
  12.1 30.2 %reduce-scatter.2.cloned.1.call-done = bf16[16,4096]{1,0:T(8,128)(2,1)} async-done(((bf16[128,4096]{1,0:T(8,128)(2,1)}), bf16[16,4096]{1,0:T(8,128)(2,1)}) %reduce-scatter.2.cloned.1.call-update) | async-done | bytes 131088 | tf_op jit(solution)/shard_map/reduce_scatter | solution.py:40
  42.3 1.1 multiply_reduce_fusion
  43.4 1.2 convolution_convert_fusion.2
  44.6 0.1 broadcast_in_dim.28
  44.7 2.0 broadcast_in_dim.29
  46.7 199.7 %all_to_all.10 = bf16[128,12,4096]{2,1,0:T(8,128)(2,1)} all-to-all(bf16[128,12,4096]{2,1,0:T(8,128)(2,1)S(1)} %bitcast.25), channel_id=1, replica_groups=mesh['dp'=16,'mp'=8] {'dp','mp'}, dimensions={0} | all-to-all | bytes 25165824 | tf_op jit(solution)/shard_map/all_to_all | solution.py:66
  246.4 18.2 %reshape.39 = bf16[1536,4096]{1,0:T(8,128)(2,1)} reshape(bf16[128,12,4096]{2,1,0:T(8,128)(2,1)} %all_to_all.10) | data formatting | bytes 25165824 | tf_op jit(solution)/shard_map/reshape | solution.py:67
  264.6 11.2 %fusion.4 = f32[1536,448]{0,1:T(8,128)} fusion(bf16[1536,4096]{1,0:T(8,128)(2,1)} %reshape.39, bf16[1,448,4096]{2,1,0:T(8,128)(2,1)} %param.15), kind=kOutput, calls=%fused_computation.9 | convolution fusion | flops 5637144576 | bytes 19005440 | tf_op jit(solution)/shard_map/dot_general | solution.py:12
  275.7 24.5 %convolution_convert_fusion = bf16[1536,4096]{1,0:T(8,128)(2,1)} fusion(bf16[1,448,4096]{2,1,0:T(8,128)(2,1)} %param.17, bf16[1536,4096]{1,0:T(8,128)(2,1)} %reshape.39, bf16[1,448,4096]{2,1,0:T(8,128)(2,1)} %param.16, f32[1536,448]{0,1:T(8,128)} %fusion.4), kind=kOutput, calls=%fused_computation.1 | convolution fusion | flops 11284709376 | bytes 35258368 | tf_op jit(solution)/shard_map/dot_general | solution.py:19
  300.2 17.9 %reshape.40 = bf16[128,12,4096]{2,1,0:T(8,128)(2,1)} reshape(bf16[1536,4096]{1,0:T(8,128)(2,1)} %convolution_convert_fusion) | data formatting | bytes 25165824 | tf_op jit(solution)/shard_map/reshape | solution.py:68
  318.1 11.0 %all-to-all-start.1 = ((bf16[128,12,4096]{2,1,0:T(8,128)(2,1)}), bf16[128,12,4096]{2,1,0:T(8,128)(2,1)}, u32[]{:S(2)}, u32[]{:S(2)}) async-start(bf16[128,12,4096]{2,1,0:T(8,128)(2,1)} %reshape.40), calls=%async_computation.2 | async-start | bytes 33554432 | tf_op jit(solution)/shard_map/all_to_all | solution.py:69
  329.2 0.1 select_reduce_fusion
  329.2 241.8 %all-to-all-done.1 = bf16[128,12,4096]{2,1,0:T(8,128)(2,1)} async-done(((bf16[128,12,4096]{2,1,0:T(8,128)(2,1)}), bf16[128,12,4096]{2,1,0:T(8,128)(2,1)}, u32[]{:S(2)}, u32[]{:S(2)}) %all-to-all-start.1) | async-done | bytes 12582944 | tf_op jit(solution)/shard_map/all_to_all | solution.py:69
  571.0 7.1 %convert_reduce_fusion = f32[4,12,4096]{2,1,0:T(8,128)S(1)} fusion(bf16[128,12,4096]{2,1,0:T(8,128)(2,1)} %all-to-all-done.1), kind=kLoop, calls=%fused_computation | loop fusion | flops 12386304 | bytes 13369344 | tf_op jit(solution)/shard_map/reduce_sum | solution.py:70
  578.1 0.1 reshape.43
  578.2 1.2 fusion
  (19 shorter events, 0.2 us)
Async XLA Ops:
  6.5 0.9 copy-start
  6.5 4.8 copy-start.5
  6.5 35.8 %copy-start.2 = (bf16[16,4096]{1,0:T(8,128)(2,1)S(1)}, bf16[16,4096]{1,0:T(8,128)(2,1)}, u32[]{:S(2)}) copy-start(bf16[16,4096]{1,0:T(8,128)(2,1)} %param.10) | copy-start | bytes 393220
  6.5 36.8 %copy-start.4 = (f32[4096]{0:T(1024)S(1)}, f32[4096]{0:T(1024)}, u32[]{:S(2)}) copy-start(f32[4096]{0:T(1024)} %param.12) | copy-start | bytes 49156
  6.5 35.7 %reduce-scatter.2.cloned.1.call-start = ((), (), s32[]{:S(2)}) async-start(), calls=%async_computation.3 | async-start | bytes 1179648 | tf_op jit(solution)/shard_map/reduce_scatter | solution.py:40
  318.1 11.0 %copy-start.6 = (f32[16,2]{0,1:T(2,128)S(1)}, f32[16,2]{0,1:T(2,128)}, u32[]{:S(2)}) copy-start(f32[16,2]{0,1:T(2,128)} %param.14) | copy-start | bytes 388
  318.1 252.9 %all-to-all-start.1 = ((bf16[128,12,4096]{2,1,0:T(8,128)(2,1)}), bf16[128,12,4096]{2,1,0:T(8,128)(2,1)}, u32[]{:S(2)}, u32[]{:S(2)}) async-start(bf16[128,12,4096]{2,1,0:T(8,128)(2,1)} %reshape.40), calls=%async_computation.2 | async-start | bytes 33554432 | tf_op jit(solution)/shard_map/all_to_all | solution.py:69
  329.2 249.0 %copy-start.3 = (bf16[16,4096]{1,0:T(8,128)(2,1)S(1)}, bf16[16,4096]{1,0:T(8,128)(2,1)}, u32[]{:S(2)}) copy-start(bf16[16,4096]{1,0:T(8,128)(2,1)} %reduce-scatter.2.cloned.1.call-done) | copy-start | bytes 393220
  571.0 8.4 %copy-start.1 = (bf16[128,512]{1,0:T(8,128)(2,1)S(1)}, bf16[128,512]{1,0:T(8,128)(2,1)}, u32[]{:S(2)}) copy-start(bf16[128,512]{1,0:T(8,128)(2,1)} %param.9) | copy-start | bytes 393220
Sparse Core Ops, SparseCore 0:
  11.5 30.7 reduce-scatter.1
where the time goes:
time: 587 us; the launch traced here: 586 us
  waiting for transfers between devices  272 us (46%)
  blocking collectives  200 us (34%)
  matrix products  41.9 us (7%)
  local copies, waits for them, and re-layouts  39.5 us (7%)
  between operations  13.5 us (2%)
  starting transfers between devices  11 us (2%)
  other arithmetic  8.63 us (1%)
    all_to_all x1, waiting for transfers between devices, body(): lax.all_to_all(pieces, ('dp', 'mp'), split_axis=0, concat_axis=0, tiled=T...  242 us
    all_to_all x1, blocking collectives, body(): lax.all_to_all(outgoing, ('dp', 'mp'), split_axis=0, concat_axis=0, tiled...  200 us
    reduce_scatter x1, waiting for transfers between devices, body(): lax.psum_scatter(jnp.dot(attn_heads, out_weight, preferred_element_type=j...  30.2 us
    dot_general x1, matrix products, expert_rows(): jnp.dot(act, down_local, preferred_element_type=jnp.float32)  24.5 us
    reshape x1, local copies, waits for them, and re-layouts, body(): received.reshape(-1, width)  18.2 us
    reshape x1, local copies, waits for them, and re-layouts, body(): pieces = result.reshape(received.shape)  17.9 us
  transfers between devices with their start and end apart: 2, of which 2 were waited for; matrix products, arithmetic and copies ran while one was open for 0% of the time, Pallas kernels for 0%

commit v1 on v0

v1 whole, which is shorter than its diff:
```python
import jax
import jax.numpy as jnp
from jax import lax
from jax.experimental import pallas as pl
from jax.experimental.pallas import tpu as pltpu
from jax.sharding import PartitionSpec as P

MESH = pl.DeviceIdType.MESH
BF = jnp.bfloat16
F32 = jnp.float32
D = 4096
CAP = 12
TOK = 16
FF = 448
BLK = 48
QUAD = 4 * BLK
GRP = 2 * QUAD
HALF = D // 2
NCH = 4
CH = D // NCH
LO = pl.ds(0, HALF)
HI = pl.ds(HALF, HALF)
NT = (((1,), (1,)), ((), ()))


def mod4(v):
    return lax.rem(v, 4)


def kernel(
    attn, resid, ow_h, gain, ids, rw, g_h, u_h, d_h, out,
    ow, wg, wu, wd, pbuf, sibp, psum, zr, hid, meta, selw, nb,
    tok, part, drecv, fq, nl, nr, fp, nlp, nrp, acc_g, acc_u, act, back, xr,
    wsem, ps_s, ps_r, z_s, z_r, m_s, m_r, x_s, x_r, a_s, a_r, b_s, b_r,
    d_s, d_r, e_s, e_r, q_s, q_r, p_s, p_r, o_s, o_r,
):
    dp = lax.axis_index("dp")
    mp = lax.axis_index("mp")
    x, y = lax.div(dp, 4), lax.rem(dp, 4)
    z, c = lax.div(mp, 2), lax.rem(mp, 2)
    o = 1 - c
    p = y * o + z * c
    q = z * o + y * c

    def at_p(k):
        t = mod4(p + k)
        return (x * 4 + t * o + q * c, (q * o + t * c) * 2 + c)

    def at_q(k):
        t = mod4(q + k)
        return (x * 4 + p * o + t * c, (t * o + p * c) * 2 + c)

    def at_x(k):
        return (mod4(x + k) * 4 + y, mp)

    def at_z(k):
        return (dp, mod4(z + k) * 2 + c)

    def at_y(k):
        return (x * 4 + mod4(y + k), mp)

    sib = (dp, z * 2 + o)
    sent = []

    def remote(src, dst, ss, rs, dev):
        return pltpu.make_async_remote_copy(
            src_ref=src, dst_ref=dst, send_sem=ss, recv_sem=rs, device_id=dev, device_id_type=MESH
        )

    def go(copy):
        copy.start()
        sent.append(copy)
        return copy

    def cols(k):
        return pl.ds(k * CH, CH)

    loads = [pltpu.make_async_copy(ow_h.at[:, cols(k)], ow.at[:, cols(k)], wsem.at[k]) for k in range(NCH)]
    experts = [
        pltpu.make_async_copy(g_h.at[0], wg, wsem.at[NCH]),
        pltpu.make_async_copy(u_h.at[0], wu, wsem.at[NCH + 1]),
        pltpu.make_async_copy(d_h.at[0], wd, wsem.at[NCH + 2]),
    ]
    for cp in loads:
        cp.start()

    lane = lax.broadcasted_iota(jnp.int32, (TOK, 128), 1)
    i_f = ids[...].astype(F32)
    w_f = rw[...]
    meta[pl.ds(0, TOK), :] = jnp.where(
        lane == 0, i_f[:, 0:1],
        jnp.where(lane == 1, i_f[:, 1:2], jnp.where(lane == 2, w_f[:, 0:1], jnp.where(lane == 3, w_f[:, 1:2], 0.0))),
    )
    meta[pl.ds(64, 64), :] = jnp.zeros((64, 128), F32)

    barrier = pltpu.get_barrier_semaphore()
    greet = [sib, at_x(1), at_x(2), at_x(3), at_z(1), at_z(2), at_z(3), at_y(1), at_y(3)]
    for dev in greet:
        pl.semaphore_signal(barrier, inc=1, device_id=dev, device_id_type=MESH)
    pl.semaphore_wait(barrier, len(greet))

    metas = [
        go(remote(meta.at[pl.ds(0, TOK)], meta.at[pl.ds((4 - k) * TOK, TOK)], m_s.at[k - 1], m_r.at[k - 1], at_x(k)))
        for k in (1, 2, 3)
    ]

    sibs = []
    for k in range(NCH):
        loads[k].wait()
        pr = jnp.dot(attn[...], ow[:, cols(k)], preferred_element_type=F32)
        pbuf[:, :, :, cols(k)] = pr.astype(BF).reshape(4, 2, TOK, CH)
        sibs.append(go(remote(pbuf.at[:, o, :, cols(k)], sibp.at[:, :, cols(k)], ps_s.at[k], ps_r.at[k], sib)))
    for cp in experts:
        cp.start()
    zs = []
    for k in range(NCH):
        sibs[k].wait_recv()
        psum[:, :, cols(k)] = (pbuf[:, c, :, cols(k)].astype(F32) + sibp[:, :, cols(k)].astype(F32)).astype(BF)
        zs.append([
            go(remote(psum.at[mod4(z + j), :, cols(k)], zr.at[j - 1, :, cols(k)], z_s.at[k, j - 1], z_r.at[k, j - 1], at_z(j)))
            for j in (1, 2, 3)
        ])
    square = jnp.zeros((TOK, 1), F32)
    for k in range(NCH):
        for cp in zs[k]:
            cp.wait_recv()
        h = resid[:, cols(k)].astype(F32) + psum[z, :, cols(k)].astype(F32)
        for j in range(3):
            h = h + zr[j, :, cols(k)].astype(F32)
        hid[:, cols(k)] = h
        square = square + jnp.sum(h * h, axis=1, keepdims=True)
    scale = lax.rsqrt(square * (1.0 / D) + 1e-05)
    xs = []
    for k in range(NCH):
        nb[pl.ds(0, TOK), cols(k)] = (hid[:, cols(k)] * scale * gain[:, cols(k)]).astype(BF)
        xs.append([
            go(remote(nb.at[pl.ds(0, TOK), cols(k)], nb.at[pl.ds((4 - j) * TOK, TOK), cols(k)], x_s.at[k, j - 1], x_r.at[k, j - 1], at_x(j)))
            for j in (1, 2, 3)
        ])

    for cp in metas:
        cp.wait_recv()
    tr = meta[...].T
    xf = x.astype(F32)
    col = lax.broadcasted_iota(jnp.int32, (8, 128), 1)
    in0 = jnp.logical_and(tr[0:1, :] == xf, col[0:1] < 64)
    in1 = jnp.logical_and(tr[1:2, :] == xf, col[0:1] < 64)
    uses = jnp.where(jnp.logical_or(in0, in1), 1.0, 0.0).astype(F32)
    weight = jnp.where(in0, tr[2:3, :], 0.0) + jnp.where(in1, tr[3:4, :], 0.0)
    ra = lax.broadcasted_iota(jnp.int32, (128, 128), 0)
    rb = lax.broadcasted_iota(jnp.int32, (128, 128), 1)
    earlier = jnp.where(jnp.logical_and(lax.div(ra, TOK) == lax.div(rb, TOK), ra < rb), 1.0, 0.0).astype(F32)
    rank = jnp.dot(jnp.broadcast_to(uses, (8, 128)), earlier, preferred_element_type=F32)
    slot = rank + (lax.div(col, TOK) * CAP).astype(F32)
    rows = lax.broadcasted_iota(jnp.int32, (BLK, 128), 0).astype(F32)
    hit = jnp.logical_and(rows == slot[0:1, :], uses > 0.5)
    sel = jnp.where(hit, 1.0, 0.0).astype(BF)[:, 0:64]
    selw[...] = jnp.where(hit, weight, 0.0)

    def blk(g, color, r):
        return tok.at[g, pl.ds(color * QUAD + r * BLK, BLK)]

    HV = (LO, HI)

    def near_p(h):
        s = blk(0, 0, 0).at[:, HV[h]]
        return [
            go(remote(s, blk(3, 0, 0).at[:, HV[h]], a_s.at[h], a_r.at[h], at_p(1))),
            go(remote(s, blk(1, 0, 0).at[:, HV[h]], a_s.at[2 + h], a_r.at[2 + h], at_p(3))),
        ]

    def near_q(g, h):
        s = blk(g, 0, 0).at[:, HV[h]]
        return [
            go(remote(s, blk(g, 0, 3).at[:, HV[h]], b_s.at[g, h], b_r.at[g, h], at_q(1))),
            go(remote(s, blk(g, 0, 1).at[:, HV[h]], b_s.at[g, 2 + h], b_r.at[g, 2 + h], at_q(3))),
        ]

    def share(g, r):
        return go(remote(blk(g, 0, r), blk(g, 1, r), d_s.at[g, r], d_r.at[g, r], sib))

    pn, qn, shared, qf = [None] * 2, [[None, None] for _ in range(4)], {}, [None] * 4
    for h in range(2):
        for k in (2 * h, 2 * h + 1):
            for cp in xs[k]:
                cp.wait_recv()
            tok[0, pl.ds(0, BLK), cols(k)] = jnp.dot(sel, nb[:, cols(k)], preferred_element_type=F32).astype(BF)
        pn[h] = near_p(h)
        qn[0][h] = near_q(0, h)
    shared[0, 0] = share(0, 0)

    def relay_q(g):
        qn[g][0][0].wait_recv()
        lo = go(remote(blk(g, 0, 3).at[:, LO], blk(g, 0, 2).at[:, LO], b_s.at[g, 4], b_r.at[g, 4], at_q(1)))
        qn[g][1][1].wait_recv()
        hi = go(remote(blk(g, 0, 1).at[:, HI], blk(g, 0, 2).at[:, HI], b_s.at[g, 5], b_r.at[g, 5], at_q(3)))
        qf[g] = (lo, hi)
        qn[g][1][0].wait_recv()
        shared[g, 3] = share(g, 3)
        qn[g][0][1].wait_recv()
        shared[g, 1] = share(g, 1)

    def far_q(g):
        qf[g][0].wait_recv()
        qf[g][1].wait_recv()
        shared[g, 2] = share(g, 2)

    def begin(g):
        for h in range(2):
            qn[g][h] = near_q(g, h)
        shared[g, 0] = share(g, 0)

    def compute(g):
        for r in (0, 3, 1, 2):
            shared[g, r].wait_recv()
        for k in range(2):
            ks = pl.ds(k * HALF, HALF)
            rows_in = tok[g, :, ks]
            gate = lax.dot_general(rows_in, wg[:, ks], NT, preferred_element_type=F32)
            if k == 0:
                acc_g[...] = gate
            else:
                acc_g[...] += gate
            up = lax.dot_general(rows_in, wu[:, ks], NT, preferred_element_type=F32)
            if k == 0:
                acc_u[...] = up
            else:
                acc_u[...] += up
        gate = acc_g[...]
        act[...] = (gate / (1.0 + jnp.exp(-gate)) * acc_u[...]).astype(BF)
        for k in range(4):
            ks = cols(k)
            part[g, :, ks] = jnp.dot(act[...], wd[:, ks], preferred_element_type=F32).astype(BF)
        return go(remote(part.at[g, pl.ds(QUAD, QUAD)], drecv.at[g], e_s.at[g], e_r.at[g], sib))

    def add(dst, srcs, at, width):
        def step(i, carry):
            ks = pl.ds(pl.multiple_of(at + i * 512, 512), 512)
            total = dst[:, ks].astype(F32)
            for s in srcs:
                total = total + s[:, ks].astype(F32)
            dst[:, ks] = total.astype(BF)
            return carry

        lax.fori_loop(0, width // 512, step, 0)

    def prt(g, r):
        return part.at[g, pl.ds(r * BLK, BLK)]

    def back_q1(g, esend):
        esend.wait_recv()
        add(part.at[g, pl.ds(0, QUAD)], [drecv.at[g]], 0, D)
        f_lo = go(remote(prt(g, 2).at[:, LO], fq.at[g, :, LO], q_s.at[g, 0], q_r.at[g, 0], at_q(1)))
        f_hi = go(remote(prt(g, 2).at[:, HI], fq.at[g, :, HI], q_s.at[g, 1], q_r.at[g, 1], at_q(3)))
        n1 = go(remote(prt(g, 1).at[:, HI], nl.at[g, :, HI], q_s.at[g, 2], q_r.at[g, 2], at_q(1)))
        n3 = go(remote(prt(g, 3).at[:, LO], nr.at[g, :, LO], q_s.at[g, 3], q_r.at[g, 3], at_q(3)))
        return [f_lo, f_hi, n1, n3]

    def back_q2(g, st):
        st[0].wait_recv()
        add(prt(g, 1), [fq.at[g]], 0, HALF)
        n1 = go(remote(prt(g, 1).at[:, LO], nl.at[g, :, LO], q_s.at[g, 4], q_r.at[g, 4], at_q(1)))
        st[1].wait_recv()
        add(prt(g, 3), [fq.at[g]], HALF, HALF)
        n3 = go(remote(prt(g, 3).at[:, HI], nr.at[g, :, HI], q_s.at[g, 5], q_r.at[g, 5], at_q(3)))
        st += [n1, n3]

    def back_q3(g, st):
        for cp in st[2:]:
            cp.wait_recv()
        add(prt(g, 0), [nl.at[g], nr.at[g]], 0, D)

    relay_q(0)
    pn[0][0].wait_recv()
    pf_lo = go(remote(blk(3, 0, 0).at[:, LO], blk(2, 0, 0).at[:, LO], a_s.at[4], a_r.at[4], at_p(1)))
    pn[1][1].wait_recv()
    pf_hi = go(remote(blk(1, 0, 0).at[:, HI], blk(2, 0, 0).at[:, HI], a_s.at[5], a_r.at[5], at_p(3)))
    pn[1][0].wait_recv()
    begin(3)
    pn[0][1].wait_recv()
    begin(1)
    far_q(0)
    pf_lo.wait_recv()
    pf_hi.wait_recv()
    begin(2)
    for cp in experts:
        cp.wait()
    e0 = compute(0)
    relay_q(3)
    relay_q(1)
    far_q(3)
    e3 = compute(3)
    relay_q(2)
    far_q(1)
    r0 = back_q1(0, e0)
    e1 = compute(1)
    far_q(2)
    back_q2(0, r0)
    r3 = back_q1(3, e3)
    e2 = compute(2)
    r1 = back_q1(1, e1)
    back_q2(3, r3)
    r2 = back_q1(2, e2)
    back_q2(1, r1)
    back_q2(2, r2)
    back_q3(2, r2)
    far_lo = go(remote(prt(2, 0).at[:, LO], fp.at[:, LO], p_s.at[0], p_r.at[0], at_p(1)))
    far_hi = go(remote(prt(2, 0).at[:, HI], fp.at[:, HI], p_s.at[1], p_r.at[1], at_p(3)))
    back_q3(1, r1)
    t1 = go(remote(prt(1, 0).at[:, HI], nlp.at[:, HI], p_s.at[2], p_r.at[2], at_p(1)))
    back_q3(3, r3)
    t3 = go(remote(prt(3, 0).at[:, LO], nrp.at[:, LO], p_s.at[3], p_r.at[3], at_p(3)))
    back_q3(0, r0)
    far_lo.wait_recv()
    add(prt(1, 0), [fp], 0, HALF)
    t1b = go(remote(prt(1, 0).at[:, LO], nlp.at[:, LO], p_s.at[4], p_r.at[4], at_p(1)))
    far_hi.wait_recv()
    add(prt(3, 0), [fp], HALF, HALF)
    t3b = go(remote(prt(3, 0).at[:, HI], nrp.at[:, HI], p_s.at[5], p_r.at[5], at_p(3)))
    for cp in (t1, t3, t1b, t3b):
        cp.wait_recv()

    ws = selw[:, 0:64]
    os_ = []
    for k in range(NCH):
        ks = cols(k)
        total = prt(0, 0)[:, ks].astype(F32) + nlp[:, ks].astype(F32) + nrp[:, ks].astype(F32)
        back[:, ks] = lax.dot_general(
            ws, total, (((0,), (0,)), ((), ())), precision=lax.Precision.HIGHEST, preferred_element_type=F32
        ).astype(BF)
        os_.append([
            go(remote(back.at[pl.ds(j * TOK, TOK), ks], xr.at[j - 1, :, ks], o_s.at[k, j - 1], o_r.at[k, j - 1], at_x(j)))
            for j in (1, 2, 3)
        ])
    for k in range(NCH):
        ks = cols(k)
        for cp in os_[k]:
            cp.wait_recv()
        total = hid[:, ks] + back[pl.ds(0, TOK), ks].astype(F32)
        for j in range(3):
            total = total + xr[j, :, ks].astype(F32)
        out[:, ks] = total.astype(BF)
    for cp in sent:
        cp.wait_send()


def body(attn_heads, residual, out_weight, norm_gain, route_ids, route_weights, gate_weights, up_weights, down_weights):
    vmem = pl.BlockSpec(memory_space=pltpu.VMEM)
    hbm = pl.BlockSpec(memory_space=pl.ANY)
    dma = pltpu.SemaphoreType.DMA
    V = pltpu.VMEM
    return pl.pallas_call(
        kernel,
        out_shape=jax.ShapeDtypeStruct((TOK, D), BF),
        in_specs=[vmem, vmem, hbm, vmem, vmem, vmem, hbm, hbm, hbm],
        out_specs=vmem,
        scratch_shapes=[
            V((512, D), BF), V((FF, D), BF), V((FF, D), BF), V((FF, D), BF),
            V((4, 2, TOK, D), BF), V((4, TOK, D), BF), V((4, TOK, D), BF), V((3, TOK, D), BF),
            V((TOK, D), F32), V((128, 128), F32), V((BLK, 128), F32), V((4 * TOK, D), BF),
            V((4, GRP, D), BF), V((4, GRP, D), BF), V((4, QUAD, D), BF),
            V((4, BLK, D), BF), V((4, BLK, D), BF), V((4, BLK, D), BF),
            V((BLK, D), BF), V((BLK, D), BF), V((BLK, D), BF),
            V((GRP, FF), F32), V((GRP, FF), F32), V((GRP, FF), BF),
            V((4 * TOK, D), BF), V((3, TOK, D), BF),
            dma((NCH + 3,)),
            dma((NCH,)), dma((NCH,)), dma((NCH, 3)), dma((NCH, 3)),
            dma((3,)), dma((3,)), dma((NCH, 3)), dma((NCH, 3)),
            dma((6,)), dma((6,)), dma((4, 6)), dma((4, 6)),
            dma((4, 4)), dma((4, 4)), dma((4,)), dma((4,)),
            dma((4, 6)), dma((4, 6)), dma((6,)), dma((6,)),
            dma((NCH, 3)), dma((NCH, 3)),
        ],
        compiler_params=pltpu.CompilerParams(
            collective_id=0, has_side_effects=True, vmem_limit_bytes=60 * 2**20
        ),
    )(attn_heads, residual, out_weight, norm_gain.reshape(1, D), route_ids, route_weights, gate_weights, up_weights, down_weights)


def solution(mesh):
    placed = (
        P("dp", "mp"),
        P(("dp", "mp"), None),
        P("mp", None),
        P(),
        P(("dp", "mp"), None),
        P(("dp", "mp"), None),
        P("dp", "mp", None),
        P("dp", "mp", None),
        P("dp", "mp", None),
    )
    return jax.shard_map(
        body, mesh=mesh, in_specs=placed, out_specs=P(("dp", "mp"), None), check_vma=False
    )
```

time: 587 us -> 122 us (0.21)
  the two profiles are of different devices: /device:TPU:50 before, /device:TPU:8 now
where the time goes in v1:
time: 122 us; the launch traced here: 120 us
  Pallas kernels  116 us (95%)
  local copies, waits for them, and re-layouts  4.27 us (3%)
    pallas_call x1, Pallas kernels, body(): pl.pallas_call(kernel, out_shape=jax.ShapeDtypeStruct((TOK, D), BF), in_s...  116 us
    unnamed x3, local copies, waits for them, and re-layouts  4.27 us

profile of v1, /device:TPU:8, one launch (start us, length us, event | category | flops | bytes accessed | tf_op | source)
XLA Modules:
  0.0 120.4 jit_solution(7805140038273103882)
XLA Ops:
  0.0 1.4 %copy.10.ids = s32[16,2]{1,0:T(8,128)} copy(s32[16,2]{0,1:T(2,128)} %param.13) | data formatting | bytes 256 | tf_op args[4]
  1.4 1.3 %copy.11.rw = f32[16,2]{1,0:T(8,128)} copy(f32[16,2]{0,1:T(2,128)} %param.14) | data formatting | bytes 256 | tf_op args[5]
  2.7 116.1 %shard_map.91 = bf16[16,4096]{1,0:T(8,128)(2,1)} custom-call(bf16[128,512]{1,0:T(8,128)(2,1)} %attn.1, bf16[16,4096]{1,0:T(8,128)(2,1)} %resid.1, bf16[512,4096]{1,0:T(8,128)(2,1)} %ow_h.1, f32[1,4096]{1,0:T(1,128)} %bitcast.1, s32[16,2]{1,0:T(8,128)} %copy.10.ids, f32[16,2]{1,0:T(8,128)} %copy.11.rw, bf16[1,448,4096]{2,1,0:T(8,128)(2,1)} %g_h.1, ...), custom_call_target="tpu_custom_call" | custom-call | tf_op jit(solution)/shard_map/pallas_call | solution.py:352
  118.8 1.6 %copy.13 = bf16[16,4096]{1,0:T(8,128)(2,1)} copy(bf16[16,4096]{1,0:T(8,128)(2,1)} %shard_map.91) | data formatting | bytes 262144

commit v2 on v1

v2 whole, which is shorter than its diff:
```python
import jax
import jax.numpy as jnp
from jax import lax
from jax.experimental import pallas as pl
from jax.experimental.pallas import tpu as pltpu
from jax.sharding import PartitionSpec as P

MESH = pl.DeviceIdType.MESH
BF = jnp.bfloat16
F32 = jnp.float32
D = 4096
CAP = 12
TOK = 16
FF = 448
BLK = 48
QUAD = 4 * BLK
GRP = 2 * QUAD
HALF = D // 2
NCH = 4
CH = D // NCH
EXT = 128
WID = EXT + D + EXT
LO = pl.ds(0, HALF)
HI = pl.ds(HALF, HALF)
HX = pl.ds(HALF, HALF + EXT)
NT = (((1,), (1,)), ((), ()))


def mod4(v):
    return lax.rem(v, 4)


def kernel(
    attn, resid, ow_h, gain, ids, rw, g_h, u_h, d_h, out,
    ow, wg, wu, wd, pbuf, sibp, zr, hid, turn, selw, onehot, nb,
    tok, part, drecv, fq, nl, nr, acc_g, acc_u, act, xr, yr,
    wsem, ps_s, ps_r, z_s, z_r, x_s, x_r, a_s, a_r, b_s, b_r,
    d_s, d_r, e_s, e_r, q_s, q_r, p_s, p_r, o_s, o_r,
):
    dp = lax.axis_index("dp")
    mp = lax.axis_index("mp")
    x, y = lax.div(dp, 4), lax.rem(dp, 4)
    z, c = lax.div(mp, 2), lax.rem(mp, 2)
    o = 1 - c
    p = y * o + z * c
    q = z * o + y * c

    def at_p(k):
        t = mod4(p + k)
        return (x * 4 + t * o + q * c, (q * o + t * c) * 2 + c)

    def at_q(k):
        t = mod4(q + k)
        return (x * 4 + p * o + t * c, (t * o + p * c) * 2 + c)

    def at_x(k):
        return (mod4(x + k) * 4 + y, mp)

    def at_z(k):
        return (dp, mod4(z + k) * 2 + c)

    def at_y(k):
        return (x * 4 + mod4(y + k), mp)

    sib = (dp, z * 2 + o)
    sent = []

    def remote(src, dst, ss, rs, dev):
        return pltpu.make_async_remote_copy(
            src_ref=src, dst_ref=dst, send_sem=ss, recv_sem=rs, device_id=dev, device_id_type=MESH
        )

    def go(copy):
        copy.start()
        sent.append(copy)
        return copy

    def cols(k):
        return pl.ds(k * CH, CH)

    loads = [pltpu.make_async_copy(ow_h.at[:, cols(k)], ow.at[:, cols(k)], wsem.at[k]) for k in range(NCH)]
    experts = [
        pltpu.make_async_copy(g_h.at[0], wg, wsem.at[NCH]),
        pltpu.make_async_copy(u_h.at[0], wu, wsem.at[NCH + 1]),
        pltpu.make_async_copy(d_h.at[0], wd, wsem.at[NCH + 2]),
    ]
    for cp in loads:
        cp.start()

    def terms(v):
        first = v.astype(BF).astype(F32)
        second = (v - first).astype(BF).astype(F32)
        return first, second, v - first - second

    turn[...] = jnp.zeros((128, 128), F32)
    turn[0:2, 0:TOK] = ids[...].astype(F32)
    for n, v in enumerate(terms(rw[...])):
        turn[2 + 2 * n : 4 + 2 * n, 0:TOK] = v
    nb[0, pl.ds(0, TOK), pl.ds(0, EXT)] = turn[...].T[0:TOK].astype(BF)
    turn[...] = jnp.zeros((128, 128), F32)

    barrier = pltpu.get_barrier_semaphore()
    greet = [sib, at_x(1), at_x(2), at_x(3), at_z(1), at_z(2), at_z(3), at_y(1), at_y(2), at_y(3)]
    for dev in greet:
        pl.semaphore_signal(barrier, inc=1, device_id=dev, device_id_type=MESH)
    for k in range(NCH):
        loads[k].wait()
        pr = jnp.dot(attn[...], ow[:, cols(k)], preferred_element_type=F32)
        pbuf[:, :, :, cols(k)] = pr.astype(BF).reshape(4, 2, TOK, CH)
    pl.semaphore_wait(barrier, len(greet))

    sibs = [
        go(remote(pbuf.at[:, o, :, cols(k)], sibp.at[:, :, cols(k)], ps_s.at[k], ps_r.at[k], sib)) for k in range(NCH)
    ]
    zs = []
    for k in range(NCH):
        sibs[k].wait_recv()
        sibp[:, :, cols(k)] = (pbuf[:, c, :, cols(k)].astype(F32) + sibp[:, :, cols(k)].astype(F32)).astype(BF)
        zs.append([
            go(remote(sibp.at[mod4(z + j), :, cols(k)], zr.at[j - 1, :, cols(k)], z_s.at[k, j - 1], z_r.at[k, j - 1], at_z(j)))
            for j in (1, 2, 3)
        ])
    def at(k):
        return pl.ds(k * CH + (EXT if k else 0), CH + (EXT if k in (0, NCH - 1) else 0))

    def body_of(k):
        return pl.ds(EXT + k * CH, CH)

    square, xs, ps = [], {}, {}

    def along_x(g, k, span):
        xs[g, k] = [
            go(remote(nb.at[g, pl.ds(0, TOK), span], nb.at[g, pl.ds((4 - j) * TOK, TOK), span], x_s.at[g, k, j - 1], x_r.at[g, k, j - 1], at_x(j)))
            for j in (1, 2, 3)
        ]

    def along_p(k):
        ps[k] = [
            go(remote(nb.at[0, pl.ds(0, TOK), at(k)], nb.at[4 - j, pl.ds(0, TOK), at(k)], a_s.at[k, j - 1], a_r.at[k, j - 1], at_p(j)))
            for j in (1, 2, 3)
        ]

    def hidden(k):
        for cp in zs[k]:
            cp.wait_recv()
        h = resid[:, cols(k)].astype(F32) + sibp[z, :, cols(k)].astype(F32)
        for j in range(3):
            h = h + zr[j, :, cols(k)].astype(F32)
        hid[:, cols(k)] = h
        square.append(jnp.sum(h * h, axis=1, keepdims=True))
        nb[0, pl.ds(0, TOK), body_of(k)] = (h * gain[:, cols(k)]).astype(BF)
        if k == NCH - 1:
            first, second, third = terms(lax.rsqrt((square[0] + square[1] + square[2] + square[3]) * (1.0 / D) + 1e-05))
            lane = lax.broadcasted_iota(jnp.int32, (TOK, EXT), 1)
            nb[0, pl.ds(0, TOK), pl.ds(EXT + D, EXT)] = jnp.where(
                lane == 0, first, jnp.where(lane == 1, second, jnp.where(lane == 2, third, 0.0))
            ).astype(BF)
        along_x(0, k, at(k))
        along_p(k)

    xf = x.astype(F32)

    def routes(g):
        turn[0 : 4 * TOK, :] = nb[g, :, pl.ds(0, EXT)].astype(F32)
        tr = turn[...].T
        col = lax.broadcasted_iota(jnp.int32, (8, 128), 1)
        in0 = jnp.logical_and(tr[0:1, :] == xf, col[0:1] < 64)
        in1 = jnp.logical_and(tr[1:2, :] == xf, col[0:1] < 64)
        uses = jnp.where(jnp.logical_or(in0, in1), 1.0, 0.0).astype(F32)
        w0 = tr[2:3, :] + tr[4:5, :] + tr[6:7, :]
        w1 = tr[3:4, :] + tr[5:6, :] + tr[7:8, :]
        weight = jnp.where(in0, w0, 0.0) + jnp.where(in1, w1, 0.0)
        ra = lax.broadcasted_iota(jnp.int32, (128, 128), 0)
        rb = lax.broadcasted_iota(jnp.int32, (128, 128), 1)
        earlier = jnp.where(jnp.logical_and(lax.div(ra, TOK) == lax.div(rb, TOK), ra < rb), 1.0, 0.0).astype(F32)
        rank = jnp.dot(jnp.broadcast_to(uses, (8, 128)), earlier, preferred_element_type=F32)
        slot = rank + (lax.div(col, TOK) * CAP).astype(F32)
        rows = lax.broadcasted_iota(jnp.int32, (BLK, 128), 0).astype(F32)
        hit = jnp.logical_and(rows == slot[0:1, :], uses > 0.5)
        selw[g] = jnp.where(hit, weight, 0.0)
        onehot[g] = jnp.where(hit, 1.0, 0.0)
        return jnp.where(hit, 1.0, 0.0).astype(BF)[:, 0:64]

    def pick(g, sel, start, width):
        tok[g, pl.ds(0, BLK), pl.ds(start, width)] = jnp.dot(
            sel, nb[g, :, pl.ds(EXT + start, width)], preferred_element_type=F32
        ).astype(BF)

    def blk(g, color, r):
        return tok.at[g, pl.ds(color * QUAD + r * BLK, BLK)]

    HV = (LO, HX)
    NV = (pl.ds(0, EXT + HALF), pl.ds(EXT + HALF, HALF + EXT))

    def near_q(g, h):
        s = blk(g, 0, 0).at[:, HV[h]]
        return [
            go(remote(s, blk(g, 0, 3).at[:, HV[h]], b_s.at[g, h], b_r.at[g, h], at_q(1))),
            go(remote(s, blk(g, 0, 1).at[:, HV[h]], b_s.at[g, 2 + h], b_r.at[g, 2 + h], at_q(3))),
        ]

    def share(g, r):
        return go(remote(blk(g, 0, r), blk(g, 1, r), d_s.at[g, r], d_r.at[g, r], sib))

    qn, shared, qf = [[None, None] for _ in range(4)], {}, [None] * 4

    def relay_q(g):
        qn[g][0][0].wait_recv()
        lo = go(remote(blk(g, 0, 3).at[:, LO], blk(g, 0, 2).at[:, LO], b_s.at[g, 4], b_r.at[g, 4], at_q(1)))
        qn[g][1][1].wait_recv()
        hi = go(remote(blk(g, 0, 1).at[:, HX], blk(g, 0, 2).at[:, HX], b_s.at[g, 5], b_r.at[g, 5], at_q(3)))
        qf[g] = (lo, hi)
        qn[g][1][0].wait_recv()
        shared[g, 3] = share(g, 3)
        qn[g][0][1].wait_recv()
        shared[g, 1] = share(g, 1)

    def far_q(g):
        qf[g][0].wait_recv()
        qf[g][1].wait_recv()
        shared[g, 2] = share(g, 2)

    def begin(g, h):
        qn[g][h] = near_q(g, h)
        if h == 1:
            shared[g, 0] = share(g, 0)

    def pass_on(h):
        for g in (3, 1, 2):
            for k in (2 * h, 2 * h + 1):
                ps[k][3 - g].wait_recv()
            along_x(g, h, NV[h])

    def enter(g):
        for h in range(2):
            for cp in xs[g, h]:
                cp.wait_recv()
            if h == 0:
                sel = routes(g)
                pick(g, sel, 0, HALF)
            else:
                pick(g, sel, HALF, HALF + EXT)
            begin(g, h)

    hidden(0)
    hidden(1)
    for cp in xs[0, 0]:
        cp.wait_recv()
    sel0 = routes(0)
    pick(0, sel0, 0, CH)
    hidden(2)
    for cp in xs[0, 1]:
        cp.wait_recv()
    pick(0, sel0, CH, CH)
    for cp in experts:
        cp.start()
    begin(0, 0)
    hidden(3)
    pass_on(0)
    for cp in xs[0, 2] + xs[0, 3]:
        cp.wait_recv()
    pick(0, sel0, HALF, HALF + EXT)
    begin(0, 1)
    pass_on(1)

    def gu(g):
        for r in (0, 3, 1, 2):
            shared[g, r].wait_recv()
        rows_in = tok[g, :, pl.ds(0, D)]
        acc_g[...] = lax.dot_general(rows_in, wg[...], NT, preferred_element_type=F32)
        acc_u[...] = lax.dot_general(rows_in, wu[...], NT, preferred_element_type=F32)
        ext = tok[g, :, pl.ds(D, EXT)].astype(F32)
        row_scale = ext[:, 0:1] + ext[:, 1:2] + ext[:, 2:3]
        gate = acc_g[...] * row_scale
        act[...] = (gate / (1.0 + jnp.exp(-gate)) * (acc_u[...] * row_scale)).astype(BF)

    def dn(g):
        for half in (1, 0):
            rs = pl.ds(half * QUAD, QUAD)
            for k in range(2):
                ks = pl.ds(k * HALF, HALF)
                part[g, rs, ks] = jnp.dot(act[rs, :], wd[:, ks], preferred_element_type=F32).astype(BF)
            if half == 1:
                passed = go(remote(part.at[g, rs], drecv.at[g], e_s.at[g], e_r.at[g], sib))
        return passed

    def add(dst, srcs, at, width):
        def step(i, carry):
            ks = pl.ds(pl.multiple_of(at + i * 512, 512), 512)
            total = dst[:, ks].astype(F32)
            for s in srcs:
                total = total + s[:, ks].astype(F32)
            dst[:, ks] = total.astype(BF)
            return carry

        lax.fori_loop(0, width // 512, step, 0)

    def prt(g, r):
        return part.at[g, pl.ds(r * BLK, BLK)]

    def back_q1(g, esend):
        esend.wait_recv()
        add(part.at[g, pl.ds(0, QUAD)], [drecv.at[g]], 0, D)
        f_lo = go(remote(prt(g, 2).at[:, LO], fq.at[g, :, LO], q_s.at[g, 0], q_r.at[g, 0], at_q(1)))
        f_hi = go(remote(prt(g, 2).at[:, HI], fq.at[g, :, HI], q_s.at[g, 1], q_r.at[g, 1], at_q(3)))
        n1 = go(remote(prt(g, 1).at[:, HI], nl.at[g, :, HI], q_s.at[g, 2], q_r.at[g, 2], at_q(1)))
        n3 = go(remote(prt(g, 3).at[:, LO], nr.at[g, :, LO], q_s.at[g, 3], q_r.at[g, 3], at_q(3)))
        return [f_lo, f_hi, n1, n3]

    def back_q2(g, st):
        st[0].wait_recv()
        add(prt(g, 1), [fq.at[g]], 0, HALF)
        n1 = go(remote(prt(g, 1).at[:, LO], nl.at[g, :, LO], q_s.at[g, 4], q_r.at[g, 4], at_q(1)))
        st[1].wait_recv()
        add(prt(g, 3), [fq.at[g]], HALF, HALF)
        n3 = go(remote(prt(g, 3).at[:, HI], nr.at[g, :, HI], q_s.at[g, 5], q_r.at[g, 5], at_q(3)))
        st += [n1, n3]

    def back_q3(g, st):
        for cp in st[2:]:
            cp.wait_recv()
        add(prt(g, 0), [nl.at[g], nr.at[g]], 0, D)

    home = {}

    def back(g, j):
        return part.at[g, pl.ds(QUAD + j * TOK, TOK)]

    def leave(g, st, passed):
        passed.wait_send()
        sent[:] = [cp for cp in sent if cp is not passed]
        for cp in st[2:]:
            cp.wait_recv()
        home[g] = []
        take = onehot[g][:, 0:64].astype(BF)
        factor = jnp.sum(selw[g], axis=1, keepdims=True)
        for k in range(2):
            for i in (2 * k, 2 * k + 1):
                ks = cols(i)
                total = prt(g, 0)[:, ks].astype(F32) + nl[g, :, ks].astype(F32) + nr[g, :, ks].astype(F32)
                part[g, pl.ds(QUAD, 4 * TOK), ks] = lax.dot_general(
                    take, (total * factor).astype(BF), (((0,), (0,)), ((), ())), preferred_element_type=F32
                ).astype(BF)
            ks = pl.ds(k * HALF, HALF)
            home[g].append([
                go(remote(back(g, j).at[:, ks], xr.at[g, j - 1, :, ks], o_s.at[g, k, j - 1], o_r.at[g, k, j - 1], at_x(j)))
                for j in (1, 2, 3)
            ])

    def over_x(g, k):
        ks = pl.ds(k * HALF, HALF)
        for cp in home[g][k]:
            cp.wait_recv()
        total = part[g, pl.ds(QUAD, TOK), ks].astype(F32)
        for j in range(3):
            total = total + xr[g, j, :, ks].astype(F32)
        return total

    ends = {}

    def onward(g):
        for k in range(2):
            ks = pl.ds(k * HALF, HALF)
            part[g, pl.ds(QUAD, TOK), ks] = over_x(g, k).astype(BF)
            ends[g, k] = go(remote(back(g, 0).at[:, ks], yr.at[3 - g, :, ks], p_s.at[g - 1, k], p_r.at[g - 1, k], at_p(g)))

    relay_q(0)
    enter(3)
    far_q(0)
    for cp in experts:
        cp.wait()
    enter(1)
    relay_q(3)
    gu(0)
    e0 = dn(0)
    enter(2)
    relay_q(1)
    far_q(3)
    gu(3)
    r0 = back_q1(0, e0)
    relay_q(2)
    e3 = dn(3)
    far_q(1)
    gu(1)
    back_q2(0, r0)
    e1 = dn(1)
    r3 = back_q1(3, e3)
    far_q(2)
    leave(0, r0, e0)
    gu(2)
    back_q2(3, r3)
    e2 = dn(2)
    r1 = back_q1(1, e1)
    leave(3, r3, e3)
    r2 = back_q1(2, e2)
    back_q2(1, r1)
    onward(3)
    back_q2(2, r2)
    leave(1, r1, e1)
    leave(2, r2, e2)
    onward(1)
    onward(2)
    for k in range(2):
        ks = pl.ds(k * HALF, HALF)
        total = hid[:, ks] + over_x(0, k)
        for g in (3, 1, 2):
            ends[g, k].wait_recv()
            total = total + yr[3 - g, :, ks].astype(F32)
        out[:, ks] = total.astype(BF)
    for cp in sent:
        cp.wait_send()


def body(attn_heads, residual, out_weight, norm_gain, route_ids, route_weights, gate_weights, up_weights, down_weights):
    vmem = pl.BlockSpec(memory_space=pltpu.VMEM)
    hbm = pl.BlockSpec(memory_space=pl.ANY)
    dma = pltpu.SemaphoreType.DMA
    V = pltpu.VMEM
    return pl.pallas_call(
        kernel,
        out_shape=jax.ShapeDtypeStruct((TOK, D), BF),
        in_specs=[vmem, vmem, hbm, vmem, vmem, vmem, hbm, hbm, hbm],
        out_specs=vmem,
        scratch_shapes=[
            V((512, D), BF), V((FF, D), BF), V((FF, D), BF), V((FF, D), BF),
            V((4, 2, TOK, D), BF), V((4, TOK, D), BF), V((3, TOK, D), BF),
            V((TOK, D), F32), V((128, 128), F32), V((4, BLK, 128), F32), V((4, BLK, 128), F32), V((4, 4 * TOK, WID), BF),
            V((4, GRP, D + EXT), BF), V((4, GRP, D), BF), V((4, QUAD, D), BF),
            V((4, BLK, D), BF), V((4, BLK, D), BF), V((4, BLK, D), BF),
            V((GRP, FF), F32), V((GRP, FF), F32), V((GRP, FF), BF),
            V((4, 3, TOK, D), BF), V((3, TOK, D), BF),
            dma((NCH + 3,)),
            dma((NCH,)), dma((NCH,)), dma((NCH, 3)), dma((NCH, 3)),
            dma((4, NCH, 3)), dma((4, NCH, 3)), dma((NCH, 3)), dma((NCH, 3)), dma((4, 6)), dma((4, 6)),
            dma((4, 4)), dma((4, 4)), dma((4,)), dma((4,)),
            dma((4, 6)), dma((4, 6)), dma((3, 2)), dma((3, 2)),
            dma((4, 2, 3)), dma((4, 2, 3)),
        ],
        compiler_params=pltpu.CompilerParams(
            collective_id=0, has_side_effects=True, vmem_limit_bytes=60 * 2**20
        ),
    )(attn_heads, residual, out_weight, norm_gain.reshape(1, D), route_ids.T, route_weights.T, gate_weights, up_weights, down_weights)


def solution(mesh):
    placed = (
        P("dp", "mp"),
        P(("dp", "mp"), None),
        P("mp", None),
        P(),
        P(("dp", "mp"), None),
        P(("dp", "mp"), None),
        P("dp", "mp", None),
        P("dp", "mp", None),
        P("dp", "mp", None),
    )
    return jax.shard_map(
        body, mesh=mesh, in_specs=placed, out_specs=P(("dp", "mp"), None), check_vma=False
    )
```

time: 122 us -> 114 us (0.934)
  Pallas kernels: 116 us -> 112 us
  local copies, waits for them, and re-layouts: 4.27 us -> 1.57 us
    pallas_call x1, Pallas kernels: 116 us -> 112 us  [body(): pl.pallas_call(kernel, out_shape=jax.ShapeDtypeStruct((TOK, D), BF), in_s...]
    unnamed x3 -> x1, local copies, waits for them, and re-layouts: 4.27 us -> 1.57 us
where the time goes in v2:
time: 114 us; the launch traced here: 113 us
  Pallas kernels  112 us (98%)
  local copies, waits for them, and re-layouts  1.57 us (1%)
    pallas_call x1, Pallas kernels, body(): pl.pallas_call(kernel, out_shape=jax.ShapeDtypeStruct((TOK, D), BF), in_s...  112 us

profile of v2, /device:TPU:8, one launch (start us, length us, event | category | flops | bytes accessed | tf_op | source)
XLA Modules:
  0.0 113.5 jit_solution(5646024448181588114)
XLA Ops:
  0.0 111.9 %shard_map.91 = bf16[16,4096]{1,0:T(8,128)(2,1)} custom-call(bf16[128,512]{1,0:T(8,128)(2,1)} %attn.1, bf16[16,4096]{1,0:T(8,128)(2,1)} %resid.1, bf16[512,4096]{1,0:T(8,128)(2,1)} %ow_h.1, f32[1,4096]{1,0:T(1,128)} %bitcast.3, s32[2,16]{1,0:T(2,128)} %bitcast.4, f32[2,16]{1,0:T(2,128)} %bitcast.5, bf16[1,448,4096]{2,1,0:T(8,128)(2,1)} %g_h.1, ...), custom_call_target="tpu_custom_call" | custom-call | tf_op jit(solution)/shard_map/pallas_call | solution.py:419
  111.9 1.6 %copy.11 = bf16[16,4096]{1,0:T(8,128)(2,1)} copy(bf16[16,4096]{1,0:T(8,128)(2,1)} %shard_map.91) | data formatting | bytes 262144

commit v3 on v2

--- a/solution.py
+++ b/solution.py
@@ -394,9 +394,9 @@
     leave(3, r3, e3)
     r2 = back_q1(2, e2)
     back_q2(1, r1)
-    onward(3)
     back_q2(2, r2)
     leave(1, r1, e1)
+    onward(3)
     leave(2, r2, e2)
     onward(1)
     onward(2)

time: 114 us -> 112 us (0.982)
  Pallas kernels: 112 us -> 110 us
    pallas_call x1, Pallas kernels: 112 us -> 110 us  [body(): pl.pallas_call(kernel, out_shape=jax.ShapeDtypeStruct((TOK, D), BF), in_s...]
where the time goes in v3:
time: 112 us
  Pallas kernels  110 us (98%)
  local copies, waits for them, and re-layouts  1.57 us (1%)
    pallas_call x1, Pallas kernels, body(): pl.pallas_call(kernel, out_shape=jax.ShapeDtypeStruct((TOK, D), BF), in_s...  110 us

profile of v3, /device:TPU:8, one launch (start us, length us, event | category | flops | bytes accessed | tf_op | source)
XLA Modules:
  0.0 112.1 jit_solution(7116299638694515375)
XLA Ops:
  0.0 110.5 %shard_map.91 = bf16[16,4096]{1,0:T(8,128)(2,1)} custom-call(bf16[128,512]{1,0:T(8,128)(2,1)} %attn.1, bf16[16,4096]{1,0:T(8,128)(2,1)} %resid.1, bf16[512,4096]{1,0:T(8,128)(2,1)} %ow_h.1, f32[1,4096]{1,0:T(1,128)} %bitcast.3, s32[2,16]{1,0:T(2,128)} %bitcast.4, f32[2,16]{1,0:T(2,128)} %bitcast.5, bf16[1,448,4096]{2,1,0:T(8,128)(2,1)} %g_h.1, ...), custom_call_target="tpu_custom_call" | custom-call | tf_op jit(solution)/shard_map/pallas_call | solution.py:419
  110.5 1.6 %copy.11 = bf16[16,4096]{1,0:T(8,128)(2,1)} copy(bf16[16,4096]{1,0:T(8,128)(2,1)} %shard_map.91) | data formatting | bytes 262144

commit v4 on v3

--- a/solution.py
+++ b/solution.py
@@ -370,8 +370,8 @@
     for cp in experts:
         cp.wait()
     enter(1)
+    gu(0)
     relay_q(3)
-    gu(0)
     e0 = dn(0)
     enter(2)
     relay_q(1)

time: 112 us -> 111 us (level); the launches traced: 112 us -> 110 us
  Pallas kernels: 110 us -> 108 us
    pallas_call x1, Pallas kernels: 110 us -> 108 us  [body(): pl.pallas_call(kernel, out_shape=jax.ShapeDtypeStruct((TOK, D), BF), in_s...]
where the time goes in v4:
time: 111 us; the launch traced here: 110 us
  Pallas kernels  108 us (97%)
  local copies, waits for them, and re-layouts  1.57 us (1%)
    pallas_call x1, Pallas kernels, body(): pl.pallas_call(kernel, out_shape=jax.ShapeDtypeStruct((TOK, D), BF), in_s...  108 us

profile of v4, /device:TPU:8, one launch (start us, length us, event | category | flops | bytes accessed | tf_op | source)
XLA Modules:
  0.0 109.7 jit_solution(17420030980233082448)
XLA Ops:
  0.0 108.2 %shard_map.91 = bf16[16,4096]{1,0:T(8,128)(2,1)} custom-call(bf16[128,512]{1,0:T(8,128)(2,1)} %attn.1, bf16[16,4096]{1,0:T(8,128)(2,1)} %resid.1, bf16[512,4096]{1,0:T(8,128)(2,1)} %ow_h.1, f32[1,4096]{1,0:T(1,128)} %bitcast.3, s32[2,16]{1,0:T(2,128)} %bitcast.4, f32[2,16]{1,0:T(2,128)} %bitcast.5, bf16[1,448,4096]{2,1,0:T(8,128)(2,1)} %g_h.1, ...), custom_call_target="tpu_custom_call" | custom-call | tf_op jit(solution)/shard_map/pallas_call | solution.py:419
  108.2 1.6 %copy.11 = bf16[16,4096]{1,0:T(8,128)(2,1)} copy(bf16[16,4096]{1,0:T(8,128)(2,1)} %shard_map.91) | data formatting | bytes 262144
